TPU v7x, 256 devices: a whole 4x4x8 slice. The times are simulated.
256 devices in a mesh: rows: 16 (over z, x_hi), cols: 16 (over x_lo, y, core).
Axes of the slice: x: 4 (x_hi: 2, x_lo: 2; x = x_hi * 2 + x_lo), y: 4, z: 8, core: 2. Of those that a mesh axis runs over, the one named last changes fastest.
Arguments:
- tokens: bfloat16 [1024, 1536, 144], P('rows', 'cols'), may hold values from -6 to 6
- norm1_gain: float32 [144], replicated, may hold values from 0.1 to 1.9
- norm1_bias: float32 [144], replicated, may hold values from -2.5 to 2.5
- qkv_weight: bfloat16 [144, 432], replicated, may hold values from -1.175 to 1.175
- qkv_bias: float32 [432], replicated, may hold values from -2.5 to 2.5
- lepe_taps: float32 [3, 144], replicated, may hold values from -3 to 3
- lepe_bias: float32 [144], replicated, may hold values from -2.5 to 2.5
- proj_weight: bfloat16 [144, 144], replicated, may hold values from -0.5 to 0.5
- proj_bias: float32 [144], replicated, may hold values from -2.5 to 2.5
- norm2_gain: float32 [144], replicated, may hold values from 0.1 to 1.9
- norm2_bias: float32 [144], replicated, may hold values from -2.5 to 2.5
- fc1_weight: bfloat16 [144, 576], replicated, may hold values from -0.5 to 0.5
- fc1_bias: float32 [576], replicated, may hold values from -2.5 to 2.5
- fc2_weight: bfloat16 [576, 144], replicated, may hold values from -0.25 to 0.25
- fc2_bias: float32 [144], replicated, may hold values from -2.5 to 2.5
Outputs:
- block_out: bfloat16 [1024, 1536, 144], P('rows', 'cols')
All inputs are finite; a program needn't handle non-finite values.
Results may differ from a plain program's by a relative error of at most 0.003.
The roundings to bfloat16 on the way count: a program that leaves them out, or rounds other values in their place, can miss the bound.
Values may be sent and summed in bfloat16 or wider, within the bound.
A program may use at most 128 MiB of HBM per device.

v0:
```python
import functools
import math

import jax
import jax.numpy as jnp
from jax import lax
from jax.experimental import pallas as pl
from jax.experimental.pallas import tpu as pltpu
from jax.sharding import PartitionSpec as P

HEADS = 3
HEAD = 24
HALF = 72
LANES = 128
F32 = jnp.float32
BF16 = jnp.bfloat16
SCALE = HEAD ** (-0.5) * math.log2(math.e)
SAFE = 80.0
NT = (((1,), (1,)), ((), ()))
TN = (((0,), (0,)), ((), ()))
VMEM = pl.BlockSpec(memory_space=pltpu.VMEM)


def pack_kernel(x_ref, eye_ref, gain_ref, bias_ref, out_ref):
    groups, per, chans = x_ref.shape
    x = x_ref[...].reshape(groups * per, chans)
    x = lax.dot_general(eye_ref[...], x, NT, preferred_element_type=F32)
    mean = jnp.mean(x, axis=0, keepdims=True)
    centred = x - mean
    variance = jnp.mean(centred * centred, axis=0, keepdims=True)
    normed = centred * lax.rsqrt(variance + 1e-05) * gain_ref[...] + bias_ref[...]
    out_ref[0] = normed.astype(BF16)


def pack(tokens, gain, bias, peers):
    length, per, chans = tokens.shape
    groups = length // peers
    const = lambda i: (0, 0)
    return pl.pallas_call(
        pack_kernel,
        grid=(peers,),
        out_shape=jax.ShapeDtypeStruct((peers, chans, groups * per), BF16),
        in_specs=[
            pl.BlockSpec((groups, per, chans), lambda i: (i, 0, 0)),
            pl.BlockSpec((chans, chans), const),
            pl.BlockSpec((chans, 1), const),
            pl.BlockSpec((chans, 1), const),
        ],
        out_specs=pl.BlockSpec((1, chans, groups * per), lambda i: (i, 0, 0)),
        cost_estimate=pl.CostEstimate(
            flops=4 * length * per * chans * chans, bytes_accessed=5 * 10**6, transcendentals=0
        ),
        name="pack",
    )(tokens, jnp.eye(chans, dtype=BF16), gain.reshape(chans, 1), bias.reshape(chans, 1))


def stripe_kernel(
    n_seq, per, qb, x_ref, w_ref, b_ref, taps_ref, lb_ref, out_ref, q_s, k_s, vt_s, vf_s, m_s
):
    peers = x_ref.shape[0]
    length = peers * per
    lane = lax.broadcasted_iota(jnp.int32, (1, LANES), 1)
    own = [(lane >= h * HEAD) & (lane < (h + 1) * HEAD) for h in range(HEADS)]
    heads = (
        lax.broadcasted_iota(jnp.int32, (LANES, LANES), 0) // HEAD
        == lax.broadcasted_iota(jnp.int32, (LANES, LANES), 1)
    ).astype(BF16)

    def project(s, tops):
        y = lax.dot_general(x_ref[s], w_ref[...], TN, preferred_element_type=F32)
        y = (y + b_ref[...]).astype(BF16)
        new = []
        for part, top in enumerate(tops):
            piece = y[:, part * LANES : (part + 1) * LANES]
            norms = jnp.dot(piece * piece, heads, preferred_element_type=F32)
            new.append(jnp.maximum(top, jnp.max(norms, axis=0, keepdims=True)))
        for i in range(n_seq):
            rows = slice(i * per, (i + 1) * per)
            dst = pl.ds(pl.multiple_of(s * per, 16), per)
            q_s[i, dst, :] = y[rows, :LANES]
            k_s[i, dst, :] = y[rows, LANES : 2 * LANES]
            dst = pl.ds(pl.multiple_of(8 + s * per, 8), per)
            vf_s[i, dst, :] = y[rows, 2 * LANES :].astype(F32)
        return tuple(new)

    for i in range(n_seq):
        vf_s[i, :8, :] = jnp.zeros((8, LANES), F32)
        vf_s[i, 8 + length :, :] = jnp.zeros((8, LANES), F32)
    zero = jnp.zeros((1, LANES), F32)
    q_top, k_top = lax.fori_loop(0, peers, project, (zero, zero))
    bound = jnp.max(q_top * k_top) * (1.05 * SCALE * SCALE)

    def turn(i, _):
        vt = vf_s[i, 8 : 8 + length, :].T
        for h in range(HEADS):
            both = [vt[h * HEAD : (h + 1) * HEAD], jnp.ones((8, length), F32)]
            vt_s[i, h] = jnp.concatenate(both, axis=0).astype(BF16)
        return 0

    lax.fori_loop(0, n_seq, turn, 0)
    blocks = length // qb

    def block(shifted, t, _):
        i = t // blocks
        at = pl.multiple_of((t % blocks) * qb, qb)
        q = q_s[i, pl.ds(at, qb), :]
        k = k_s[i]
        parts = []
        for h in range(HEADS):
            qh = jnp.where(own[h], q, jnp.zeros_like(q))
            s = lax.dot_general(k, qh, NT, preferred_element_type=F32)
            if shifted:
                s = s - jnp.max(s, axis=0, keepdims=True)
            p = jnp.exp2(s * SCALE).astype(BF16)
            o = jnp.dot(vt_s[i, h], p, preferred_element_type=F32)
            parts.append(o[:HEAD] / o[HEAD : HEAD + 1])
        parts.append(jnp.zeros((LANES - HALF, qb), F32))
        att = jnp.concatenate(parts, axis=0).T.astype(BF16).astype(F32)
        lepe = (
            taps_ref[0:1] * vf_s[i, pl.ds(at + 7, qb), :]
            + taps_ref[1:2] * vf_s[i, pl.ds(at + 8, qb), :]
            + taps_ref[2:3] * vf_s[i, pl.ds(at + 9, qb), :]
            + lb_ref[...]
        )
        m_s[i, pl.ds(at, qb), :] = att + lepe
        return 0

    safe = bound < SAFE * SAFE

    @pl.when(safe)
    def _():
        lax.fori_loop(0, n_seq * blocks, functools.partial(block, False), 0)

    @pl.when(jnp.logical_not(safe))
    def _():
        lax.fori_loop(0, n_seq * blocks, functools.partial(block, True), 0)

    def send(d, _):
        x = m_s[:, pl.ds(pl.multiple_of(d * per, 16), per), :].reshape(n_seq * per, LANES)
        out_ref[d] = x.T[:HALF].astype(BF16)
        return 0

    lax.fori_loop(0, peers, send, 0)


def stripe(received, weight, bias, taps, lepe_bias, per, qb):
    peers, _, width = received.shape
    n_seq = width // per
    length = peers * per
    return pl.pallas_call(
        functools.partial(stripe_kernel, n_seq, per, qb),
        out_shape=jax.ShapeDtypeStruct((peers, HALF, width), BF16),
        in_specs=[VMEM] * 5,
        out_specs=VMEM,
        scratch_shapes=[
            pltpu.VMEM((n_seq, length, LANES), BF16),
            pltpu.VMEM((n_seq, length, LANES), BF16),
            pltpu.VMEM((n_seq, HEADS, 32, length), BF16),
            pltpu.VMEM((n_seq, length + 16, LANES), F32),
            pltpu.VMEM((n_seq, length, LANES), F32),
        ],
        compiler_params=pltpu.CompilerParams(vmem_limit_bytes=50 * 2**20),
        cost_estimate=pl.CostEstimate(
            flops=4 * HEADS * n_seq * length * length * 256,
            bytes_accessed=4 * 10**6,
            transcendentals=HEADS * n_seq * length * length,
        ),
        name="stripe",
    )(received, weight, bias, taps, lepe_bias)


def tail_kernel(
    x_ref, row_ref, col_ref, eye_ref, wr_ref, wc_ref, pb_ref, g_ref, b_ref,
    f1_ref, f1b_ref, f2_ref, f2b_ref, out_ref, col_s,
):
    rows, tile_w, chans = x_ref.shape
    peers, _, width = col_ref.shape
    tile_h = rows * peers
    per = width // tile_h

    @pl.when(pl.program_id(0) == 0)
    def _():
        for r in range(peers):
            y = lax.dot_general(col_ref[r], eye_ref[...], TN, preferred_element_type=F32)
            for j in range(per):
                col_s[pl.ds(r * per + j, tile_h, stride=tile_w), :] = y[j * tile_h : (j + 1) * tile_h]

    count = rows * tile_w
    at = pl.multiple_of(pl.program_id(0) * count, count)
    col = col_s[pl.ds(at, count), :].astype(BF16)
    resid = (
        x_ref[...].reshape(count, chans).astype(F32)
        + lax.dot_general(row_ref[0], wr_ref[...], TN, preferred_element_type=F32)
        + jnp.dot(col, wc_ref[...], preferred_element_type=F32)
        + pb_ref[...]
    )
    mean = jnp.mean(resid, axis=-1, keepdims=True)
    centred = resid - mean
    variance = jnp.mean(centred * centred, axis=-1, keepdims=True)
    normed = (centred * lax.rsqrt(variance + 1e-05) * g_ref[...] + b_ref[...]).astype(BF16)
    hidden = jnp.dot(normed, f1_ref[...], preferred_element_type=F32) + f1b_ref[...]
    hidden = (0.5 * hidden * (1.0 + lax.erf(hidden * (0.5**0.5)))).astype(BF16)
    out = resid + jnp.dot(hidden, f2_ref[...], preferred_element_type=F32) + f2b_ref[...]
    out_ref[...] = out.astype(BF16).reshape(rows, tile_w, chans)


def tail(tokens, row, col, proj_w, proj_b, gain, bias, fc1_w, fc1_b, fc2_w, fc2_b):
    tile_h, tile_w, chans = tokens.shape
    peers, _, width = row.shape
    rows = tile_h // peers
    ffn = fc1_w.shape[1]
    const2 = lambda i: (0, 0)
    full = lambda a: pl.BlockSpec(a.shape, lambda i: (0,) * a.ndim)
    wc = jnp.pad(proj_w[HALF:], ((0, LANES - HALF), (0, 0)))
    consts = [
        jnp.eye(HALF, LANES, dtype=BF16), proj_w[:HALF], wc, proj_b[None], gain[None], bias[None],
        fc1_w, fc1_b[None], fc2_w, fc2_b[None],
    ]
    return pl.pallas_call(
        tail_kernel,
        grid=(peers,),
        out_shape=jax.ShapeDtypeStruct(tokens.shape, BF16),
        in_specs=[
            pl.BlockSpec((rows, tile_w, chans), lambda i: (i, 0, 0)),
            pl.BlockSpec((1, HALF, width), lambda i: (i, 0, 0)),
            full(col),
        ] + [full(a) for a in consts],
        out_specs=pl.BlockSpec((rows, tile_w, chans), lambda i: (i, 0, 0)),
        scratch_shapes=[pltpu.VMEM((tile_h * tile_w, LANES), F32)],
        compiler_params=pltpu.CompilerParams(vmem_limit_bytes=50 * 2**20),
        cost_estimate=pl.CostEstimate(
            flops=2 * tile_h * tile_w * chans * (chans + 2 * ffn),
            bytes_accessed=8 * 10**6,
            transcendentals=tile_h * tile_w * ffn,
        ),
        name="tail",
    )(tokens, row, col, *consts)


def shards(
    tokens, norm1_gain, norm1_bias, qkv_weight, qkv_bias, lepe_taps, lepe_bias, proj_weight,
    proj_bias, norm2_gain, norm2_bias, fc1_weight, fc1_bias, fc2_weight, fc2_bias,
):
    tile_h, tile_w, chans = tokens.shape
    n_rows = lax.axis_size("rows")
    n_cols = lax.axis_size("cols")

    def branch(which):
        lo = which * HALF
        lanes = lambda a: jnp.pad(a, [(0, 0)] * (a.ndim - 1) + [(0, LANES - HALF)])
        cut = lambda a: jnp.concatenate(
            [lanes(a[..., b * chans + lo : b * chans + lo + HALF]) for b in range(3)], axis=-1
        )
        return (
            cut(qkv_weight),
            cut(qkv_bias)[None],
            lanes(lepe_taps[:, lo : lo + HALF]),
            lanes(lepe_bias[lo : lo + HALF])[None],
        )

    swap = lambda a, axis: lax.all_to_all(a, axis, split_axis=0, concat_axis=0, tiled=True)
    row_in = swap(pack(tokens, norm1_gain, norm1_bias, n_cols), "cols")
    col_in = swap(pack(jnp.swapaxes(tokens, 0, 1), norm1_gain, norm1_bias, n_rows), "rows")
    row_out = swap(stripe(row_in, *branch(0), tile_w, 768), "cols")
    col_out = swap(stripe(col_in, *branch(1), tile_h, 1024), "rows")
    return tail(
        tokens, row_out, col_out, proj_weight, proj_bias, norm2_gain, norm2_bias,
        fc1_weight, fc1_bias, fc2_weight, fc2_bias,
    )


def solution(mesh):
    in_specs = (P("rows", "cols", None),) + (P(),) * 14
    return jax.shard_map(
        shards, mesh=mesh, in_specs=in_specs, out_specs=P("rows", "cols", None), check_vma=False
    )
```

profile of v0, /device:TPU:8, one launch (start us, length us, event | category | flops | bytes accessed | tf_op | source)
XLA Modules:
  0.0 223.9 jit_solution(3878139180522352296)
XLA Ops:
  0.0 0.6 fusion.6.eye_ref
  0.6 1.4 copy.22.gain_ref
  2.1 1.4 copy.23.bias_ref
  3.5 4.6 %copy.27.x_ref = bf16[64,96,144]{2,1,0:T(8,128)(2,1)} copy(bf16[64,96,144]{1,2,0:T(8,128)(2,1)} %param.15) | data formatting | bytes 3538944 | tf_op args[0]
  8.1 11.7 %pack.2 = bf16[16,144,384]{2,1,0:T(8,128)(2,1)} custom-call(bf16[64,96,144]{2,1,0:T(8,128)(2,1)} %copy.27.x_ref, bf16[144,144]{1,0:T(8,128)(2,1)} %fusion.6.eye_ref, f32[144,1]{1,0:T(8,128)} %copy.22.gain_ref, f32[144,1]{1,0:T(8,128)} %copy.23.bias_ref), custom_call_target="tpu_custom_call" | custom-call | flops 509607936 | bytes 5000000 | tf_op jit(solution)/shard_map/pack/pallas_call | solution.py:39
  19.8 5.9 %all-to-all-start = ((bf16[16,144,384]{2,1,0:T(8,128)(2,1)}), bf16[16,144,384]{2,1,0:T(8,128)(2,1)S(1)}, u32[]{:S(2)}, u32[]{:S(2)}) async-start(bf16[16,144,384]{2,1,0:T(8,128)(2,1)} %pack.2), calls=%async_computation | async-start | bytes 3538944 | tf_op jit(solution)/shard_map/all_to_all | solution.py:261
  25.6 0.0 copy-start.12
  25.6 6.5 %copy.24 = bf16[64,96,144]{2,0,1:T(8,128)(2,1)} copy(bf16[64,96,144]{1,2,0:T(8,128)(2,1)} %param.15) | data formatting | bytes 3538944 | tf_op args[0]
  32.2 0.0 copy-done.12
  32.2 0.1 slice.73
  32.2 0.0 copy-start.10
  32.2 0.0 copy-start.9
  32.2 0.0 copy-start.8
  32.2 11.8 %pack.3 = bf16[16,144,384]{2,1,0:T(8,128)(2,1)} custom-call(bf16[96,64,144]{2,1,0:T(8,128)(2,1)} %bitcast.15, bf16[144,144]{1,0:T(8,128)(2,1)} %fusion.6.eye_ref, f32[144,1]{1,0:T(8,128)} %copy.22.gain_ref, f32[144,1]{1,0:T(8,128)} %copy.23.bias_ref), custom_call_target="tpu_custom_call" | custom-call | flops 509607936 | bytes 5000000 | tf_op jit(solution)/shard_map/pack/pallas_call | solution.py:39
  44.0 0.0 copy-done.10
  44.0 0.1 fusion.15
  44.1 0.0 copy-done.9
  44.1 0.6 select_maximum_fusion.2
  44.7 0.0 copy-done.8
  44.7 0.7 fusion.13
  45.5 0.7 fusion.10.w_ref
  46.1 2.2 all-to-all-done.x_ref
  48.3 10.7 %all-to-all-start.2 = ((bf16[16,144,384]{2,1,0:T(8,128)(2,1)}), bf16[16,144,384]{2,1,0:T(8,128)(2,1)S(1)}, u32[]{:S(2)}, u32[]{:S(2)}) async-start(bf16[16,144,384]{2,1,0:T(8,128)(2,1)} %pack.3), calls=%async_computation.2 | async-start | bytes 3538944 | tf_op jit(solution)/shard_map/all_to_all | solution.py:261
  59.1 0.8 slice.72
  59.8 0.7 broadcast_in_dim.27.b_ref
  60.5 0.8 slice_select_fusion
  61.3 0.8 fusion.8.w_ref
  62.1 0.7 slice_select_fusion.1.taps_ref
  62.8 49.6 %stripe.2 = bf16[16,72,384]{2,1,0:T(8,128)(2,1)S(1)} custom-call(bf16[16,144,384]{2,1,0:T(8,128)(2,1)S(1)} %all-to-all-done.x_ref, bf16[144,384]{1,0:T(8,128)(2,1)S(1)} %fusion.8.w_ref, f32[1,384]{1,0:T(1,128)S(1)} %broadcast_in_dim.27.b_ref, f32[3,128]{1,0:T(4,128)S(1)} %slice_select_fusion.1.taps_ref, f32[1,128]{1,0:T(1,128)S(1)} %get-tuple-element.17.lb_ref), custom_call_target="tpu_custom_call" | custom-call | flops 28991029248 | bytes 4000000 | tf_op jit(solution)/shard_map/stripe/pallas_call | solution.py:150
  112.4 0.0 copy-start.1
  112.4 0.9 copy-done.1
  113.3 0.0 all-to-all-done.2.x_ref
  113.3 6.6 %all-to-all-start.1 = ((bf16[16,72,384]{2,1,0:T(8,128)(2,1)}), bf16[16,72,384]{2,1,0:T(8,128)(2,1)S(1)}, u32[]{:S(2)}, u32[]{:S(2)}) async-start(bf16[16,72,384]{2,1,0:T(8,128)(2,1)} %copy-done.1), calls=%async_computation.1 | async-start | bytes 1769472 | tf_op jit(solution)/shard_map/all_to_all | solution.py:261
  119.9 0.0 copy-start.3
  119.9 0.9 copy-done.3
  120.8 0.0 copy-start.11
  120.8 37.5 %stripe.3 = bf16[16,72,384]{2,1,0:T(8,128)(2,1)S(1)} custom-call(bf16[16,144,384]{2,1,0:T(8,128)(2,1)S(1)} %all-to-all-done.2.x_ref, bf16[144,384]{1,0:T(8,128)(2,1)S(1)} %copy-done.3, f32[1,384]{1,0:T(1,128)S(1)} %broadcast_in_dim.29.b_ref, f32[3,128]{1,0:T(4,128)S(1)} %pad.69.taps_ref, f32[1,128]{1,0:T(1,128)S(1)} %pad_bitcast_fusion.lb_ref), custom_call_target="tpu_custom_call" | custom-call | flops 19327352832 | bytes 4000000 | tf_op jit(solution)/shard_map/stripe/pallas_call | solution.py:150
  158.3 0.0 copy-start
  158.3 0.9 copy-done
  159.2 0.0 copy-start.2
  159.2 0.0 copy-start.4
  159.2 0.0 copy-start.5
  159.2 0.0 copy-start.6
  159.2 0.0 copy-start.7
  159.3 0.0 all-to-all-done.1.row_ref
  159.3 10.0 %all-to-all-start.3 = ((bf16[16,72,384]{2,1,0:T(8,128)(2,1)}), bf16[16,72,384]{2,1,0:T(8,128)(2,1)S(1)}, u32[]{:S(2)}, u32[]{:S(2)}) async-start(bf16[16,72,384]{2,1,0:T(8,128)(2,1)} %copy-done), calls=%async_computation.3 | async-start | bytes 1769472 | tf_op jit(solution)/shard_map/all_to_all | solution.py:261
  169.2 1.1 copy.28.f2_ref
  170.3 0.0 copy-done.11
  170.3 0.8 fusion.14
  171.2 25.2 %all-to-all-done.3.col_ref = bf16[16,72,384]{2,1,0:T(8,128)(2,1)S(1)} async-done(((bf16[16,72,384]{2,1,0:T(8,128)(2,1)}), bf16[16,72,384]{2,1,0:T(8,128)(2,1)S(1)}, u32[]{:S(2)}, u32[]{:S(2)}) %all-to-all-start.3) | async-done | bytes 884768 | tf_op jit(solution)/shard_map/all_to_all | solution.py:261
  196.4 0.0 copy-done.2
  196.4 0.0 copy-done.4
  196.4 0.0 copy-done.5
  196.4 0.0 copy-done.6
  196.4 0.0 copy-done.7
  196.4 22.9 %tail.1 = bf16[64,96,144]{2,1,0:T(8,128)(2,1)} custom-call(bf16[64,96,144]{2,1,0:T(8,128)(2,1)} %copy.27.x_ref, bf16[16,72,384]{2,1,0:T(8,128)(2,1)S(1)} %all-to-all-done.1.row_ref, bf16[16,72,384]{2,1,0:T(8,128)(2,1)S(1)} %all-to-all-done.3.col_ref, bf16[72,128]{1,0:T(8,128)(2,1)S(1)} %fusion.11.eye_ref, bf16[72,144]{1,0:T(8,128)(2,1)S(1)} %get-tuple-element.11.wr_ref, ...), custom_call_target="tpu_custom_call" | custom-call | flops 2293235712 | bytes 8000000 | tf_op jit(solution)/shard_map/tail/pallas_call | solution.py:219
  219.3 4.6 %copy.29 = bf16[64,96,144]{1,2,0:T(8,128)(2,1)} copy(bf16[64,96,144]{2,1,0:T(8,128)(2,1)} %tail.1) | data formatting | bytes 3538944 | tf_op jit(solution)/shard_map/tail/pallas_call | solution.py:219
  (8 shorter events, 0.1 us)
Async XLA Ops:
  19.8 28.5 %all-to-all-start = ((bf16[16,144,384]{2,1,0:T(8,128)(2,1)}), bf16[16,144,384]{2,1,0:T(8,128)(2,1)S(1)}, u32[]{:S(2)}, u32[]{:S(2)}) async-start(bf16[16,144,384]{2,1,0:T(8,128)(2,1)} %pack.2), calls=%async_computation | async-start | bytes 3538944 | tf_op jit(solution)/shard_map/all_to_all | solution.py:261
  25.6 6.5 %copy-start.12 = (f32[144]{0:T(256)S(1)}, f32[144]{0:T(256)}, u32[]{:S(2)}) copy-start(f32[144]{0:T(256)} %param.21) | copy-start | bytes 1732
  32.2 11.8 %copy-start.10 = (f32[432]{0:T(512)S(1)}, f32[432]{0:T(512)}, u32[]{:S(2)}) copy-start(f32[432]{0:T(512)} %param.19) | copy-start | bytes 5188
  32.2 11.9 %copy-start.9 = (pred[128]{0:T(512)(128)(4,1)S(1)}, pred[128]{0:T(512)(128)(4,1)}, u32[]{:S(2)}) copy-start(pred[128]{0:T(512)(128)(4,1)} %constant.7.clone.1) | copy-start | bytes 388
  32.2 12.5 %copy-start.8 = (bf16[144,432]{1,0:T(8,128)(2,1)S(1)}, bf16[144,432]{1,0:T(8,128)(2,1)}, u32[]{:S(2)}) copy-start(bf16[144,432]{1,0:T(8,128)(2,1)} %param.18) | copy-start | bytes 373252
  48.3 65.0 %all-to-all-start.2 = ((bf16[16,144,384]{2,1,0:T(8,128)(2,1)}), bf16[16,144,384]{2,1,0:T(8,128)(2,1)S(1)}, u32[]{:S(2)}, u32[]{:S(2)}) async-start(bf16[16,144,384]{2,1,0:T(8,128)(2,1)} %pack.3), calls=%async_computation.2 | async-start | bytes 3538944 | tf_op jit(solution)/shard_map/all_to_all | solution.py:261
  112.4 0.9 copy-start.1
  113.3 45.9 %all-to-all-start.1 = ((bf16[16,72,384]{2,1,0:T(8,128)(2,1)}), bf16[16,72,384]{2,1,0:T(8,128)(2,1)S(1)}, u32[]{:S(2)}, u32[]{:S(2)}) async-start(bf16[16,72,384]{2,1,0:T(8,128)(2,1)} %copy-done.1), calls=%async_computation.1 | async-start | bytes 1769472 | tf_op jit(solution)/shard_map/all_to_all | solution.py:261
  119.9 0.9 copy-start.3
  120.8 49.5 %copy-start.11 = (f32[576]{0:T(1024)S(1)}, f32[576]{0:T(1024)}, u32[]{:S(2)}) copy-start(f32[576]{0:T(1024)} %param.27) | copy-start | bytes 6916
  158.3 0.9 copy-start
  159.2 37.1 %copy-start.2 = (bf16[144,576]{1,0:T(8,128)(2,1)S(1)}, bf16[144,576]{1,0:T(8,128)(2,1)}, u32[]{:S(2)}) copy-start(bf16[144,576]{1,0:T(8,128)(2,1)} %f1_ref.1) | copy-start | bytes 497668
  159.2 37.1 %copy-start.4 = (f32[144]{0:T(256)S(1)}, f32[144]{0:T(256)}, u32[]{:S(2)}) copy-start(f32[144]{0:T(256)} %param.23) | copy-start | bytes 1732
  159.2 37.1 %copy-start.5 = (f32[144]{0:T(256)S(1)}, f32[144]{0:T(256)}, u32[]{:S(2)}) copy-start(f32[144]{0:T(256)} %param.24) | copy-start | bytes 1732
  159.2 37.1 %copy-start.6 = (f32[144]{0:T(256)S(1)}, f32[144]{0:T(256)}, u32[]{:S(2)}) copy-start(f32[144]{0:T(256)} %param.25) | copy-start | bytes 1732
  159.2 37.1 %copy-start.7 = (f32[144]{0:T(256)S(1)}, f32[144]{0:T(256)}, u32[]{:S(2)}) copy-start(f32[144]{0:T(256)} %param.29) | copy-start | bytes 1732
  159.3 37.1 %all-to-all-start.3 = ((bf16[16,72,384]{2,1,0:T(8,128)(2,1)}), bf16[16,72,384]{2,1,0:T(8,128)(2,1)S(1)}, u32[]{:S(2)}, u32[]{:S(2)}) async-start(bf16[16,72,384]{2,1,0:T(8,128)(2,1)} %copy-done), calls=%async_computation.3 | async-start | bytes 1769472 | tf_op jit(solution)/shard_map/all_to_all | solution.py:261
where the time goes:
time: 225 us; the launch traced here: 224 us
  Pallas kernels  133 us (59%)
  starting transfers between devices  33.1 us (15%)
  waiting for transfers between devices  27.4 us (12%)
  local copies, waits for them, and re-layouts  25.5 us (11%)
  other arithmetic  4.2 us (2%)
    pallas_call x2, Pallas kernels, stripe(): pl.pallas_call(functools.partial(stripe_kernel, n_seq, per, qb), out_shap...  87.1 us
    all_to_all x4, starting transfers between devices, shards(): lax.all_to_all(a, axis, split_axis=0, concat_axis=0, tiled=True)  33.1 us
    all_to_all x4, waiting for transfers between devices, shards(): lax.all_to_all(a, axis, split_axis=0, concat_axis=0, tiled=True)  27.4 us
    pallas_call x2, Pallas kernels, pack(): pl.pallas_call(pack_kernel, grid=(peers,), out_shape=jax.ShapeDtypeStruct...  23.5 us
    pallas_call x1, Pallas kernels, tail(): pl.pallas_call(tail_kernel, grid=(peers,), out_shape=jax.ShapeDtypeStruct...  22.9 us
    unnamed x29, local copies, waits for them, and re-layouts  15 us
    pallas_call x1, local copies, waits for them, and re-layouts, tail(): pl.pallas_call(tail_kernel, grid=(peers,), out_shape=jax.ShapeDtypeStruct...  4.6 us
  transfers between devices with their start and end apart: 4, of which 2 were waited for; matrix products, arithmetic and copies ran while one was open for 6% of the time, Pallas kernels for 44%

commit v1 on v0

v1 whole, which is shorter than its diff:
```python
import functools
import math

import jax
import jax.numpy as jnp
from jax import lax
from jax.experimental import pallas as pl
from jax.experimental.pallas import tpu as pltpu
from jax.sharding import PartitionSpec as P

HEADS = 3
HEAD = 24
HALF = 72
LANES = 128
F32 = jnp.float32
BF16 = jnp.bfloat16
SCALE = HEAD ** (-0.5) * math.log2(math.e)
SAFE = 80.0
UNROLL = 4
NT = (((1,), (1,)), ((), ()))
TN = (((0,), (0,)), ((), ()))
VMEM = pl.BlockSpec(memory_space=pltpu.VMEM)


def columns(row, lanes):
    return jnp.broadcast_to(row, (lanes, row.shape[1])).T


def norm_channels(x, gain, bias):
    mean = jnp.mean(x, axis=0, keepdims=True)
    centred = x - mean
    variance = jnp.mean(centred * centred, axis=0, keepdims=True)
    return centred * lax.rsqrt(variance + 1e-05) * gain + bias


def pack_rows_kernel(x_ref, gain_ref, bias_ref, out_ref):
    rows, chans, cols = x_ref.shape
    gain = columns(gain_ref[...], cols)
    bias = columns(bias_ref[...], cols)
    peers = out_ref.shape[0]
    each = rows // peers

    def turn(p, _):
        xs = [
            norm_channels(x_ref[p * each + i].astype(F32), gain, bias) for i in range(each)
        ]
        out_ref[p] = jnp.concatenate(xs, axis=1).astype(BF16)
        return 0

    lax.fori_loop(0, peers, turn, 0, unroll=2)


def pack_cols_kernel(x_ref, gain_ref, bias_ref, out_ref, turned):
    rows, chans, cols = x_ref.shape
    peers, _, width = out_ref.shape
    spot = lambda shape: lax.broadcasted_iota(jnp.int32, shape, 0) == lax.broadcasted_iota(
        jnp.int32, shape, 1
    )
    wide = spot((chans, 2 * LANES)).astype(BF16)
    eye = spot((chans, chans)).astype(BF16)
    gain = columns(gain_ref[...], cols)
    bias = columns(bias_ref[...], cols)
    step = 16

    def turn(g, _):
        ys = []
        for i in range(step):
            x = norm_channels(x_ref[g * step + i].astype(F32), gain, bias)
            ys.append(lax.dot_general(x.astype(BF16), wide, TN, preferred_element_type=F32))
        at = pl.ds(pl.multiple_of(g * step, step), step)
        turned[:, at, :] = jnp.swapaxes(jnp.stack(ys), 0, 1)
        return 0

    lax.fori_loop(0, rows // step, turn, 0)
    per = width // rows

    def write(p, _):
        x = turned[pl.ds(p * per, per)].reshape(width, 2 * LANES)[:, :chans].astype(BF16)
        out = lax.dot_general(eye, x, NT, preferred_element_type=F32)
        out_ref[p] = out.astype(BF16)
        return 0

    lax.fori_loop(0, peers, write, 0, unroll=4)


def pack(kernel, scratch, name, tokens, gain, bias, peers):
    rows, chans, cols = tokens.shape
    return pl.pallas_call(
        kernel,
        out_shape=jax.ShapeDtypeStruct((peers, chans, rows * cols // peers), BF16),
        in_specs=[VMEM] * 3,
        out_specs=VMEM,
        scratch_shapes=scratch,
        compiler_params=pltpu.CompilerParams(vmem_limit_bytes=40 * 2**20),
        cost_estimate=pl.CostEstimate(
            flops=10**10, bytes_accessed=5 * 10**6, transcendentals=0
        ),
        name=name,
    )(tokens, gain[None], bias[None])


def stripe_kernel(
    first, n_seq, per, qb, x_ref, w_ref, b_ref, taps_ref, lb_ref, out_ref,
    q_s, k_s, vt_s, vf_s, m_s,
):
    peers = x_ref.shape[0]
    length = peers * per
    lane = lax.broadcasted_iota(jnp.int32, (1, LANES), 1)
    own = [(lane >= h * HEAD) & (lane < (h + 1) * HEAD) for h in range(HEADS)]
    heads = (
        lax.broadcasted_iota(jnp.int32, (LANES, LANES), 0) // HEAD
        == lax.broadcasted_iota(jnp.int32, (LANES, LANES), 1)
    ).astype(BF16)

    def project(s, tops):
        x = x_ref[s][:, first * per : (first + n_seq) * per]
        y = lax.dot_general(x, w_ref[...], TN, preferred_element_type=F32)
        y = (y + b_ref[...]).astype(BF16)
        new = []
        for part, top in enumerate(tops):
            piece = y[:, part * LANES : (part + 1) * LANES]
            norms = jnp.dot(piece * piece, heads, preferred_element_type=F32)
            new.append(jnp.maximum(top, jnp.max(norms, axis=0, keepdims=True)))
        for i in range(n_seq):
            rows = slice(i * per, (i + 1) * per)
            dst = pl.ds(pl.multiple_of(s * per, 16), per)
            q_s[i, dst, :] = y[rows, :LANES]
            k_s[i, dst, :] = y[rows, LANES : 2 * LANES]
            dst = pl.ds(pl.multiple_of(8 + s * per, 8), per)
            vf_s[i, dst, :] = y[rows, 2 * LANES :].astype(F32)
        return tuple(new)

    for i in range(n_seq):
        vf_s[i, :8, :] = jnp.zeros((8, LANES), F32)
        vf_s[i, 8 + length :, :] = jnp.zeros((8, LANES), F32)
    zero = jnp.zeros((1, LANES), F32)
    q_top, k_top = lax.fori_loop(0, peers, project, (zero, zero), unroll=UNROLL)
    bound = jnp.max(q_top * k_top) * (1.05 * SCALE * SCALE)

    def turn(i, _):
        vt = vf_s[i, 8 : 8 + length, :].T
        for h in range(HEADS):
            both = [vt[h * HEAD : (h + 1) * HEAD], jnp.ones((8, length), F32)]
            vt_s[i, h] = jnp.concatenate(both, axis=0).astype(BF16)
        return 0

    lax.fori_loop(0, n_seq, turn, 0)
    blocks = length // qb

    def block(shifted, t, _):
        i = t // blocks
        at = pl.multiple_of((t % blocks) * qb, qb)
        q = q_s[i, pl.ds(at, qb), :]
        k = k_s[i]
        parts = []
        for h in range(HEADS):
            qh = jnp.where(own[h], q, jnp.zeros_like(q))
            s = lax.dot_general(k, qh, NT, preferred_element_type=F32)
            if shifted:
                s = s - jnp.max(s, axis=0, keepdims=True)
            p = jnp.exp2(s * SCALE).astype(BF16)
            o = jnp.dot(vt_s[i, h], p, preferred_element_type=F32)
            parts.append(o[:HEAD] / o[HEAD : HEAD + 1])
        parts.append(jnp.zeros((LANES - HALF, qb), F32))
        att = jnp.concatenate(parts, axis=0).T.astype(BF16).astype(F32)
        lepe = (
            taps_ref[0:1] * vf_s[i, pl.ds(at + 7, qb), :]
            + taps_ref[1:2] * vf_s[i, pl.ds(at + 8, qb), :]
            + taps_ref[2:3] * vf_s[i, pl.ds(at + 9, qb), :]
            + lb_ref[...]
        )
        m_s[i, pl.ds(at, qb), :] = att + lepe
        return 0

    safe = bound < SAFE * SAFE

    @pl.when(safe)
    def _():
        lax.fori_loop(0, n_seq * blocks, functools.partial(block, False), 0)

    @pl.when(jnp.logical_not(safe))
    def _():
        lax.fori_loop(0, n_seq * blocks, functools.partial(block, True), 0)

    def send(d, _):
        at = pl.ds(pl.multiple_of(d * per, 16), per)
        out_ref[d] = m_s[:, at, :].reshape(n_seq * per, LANES).T[:HALF].astype(BF16)
        return 0

    lax.fori_loop(0, peers, send, 0, unroll=UNROLL)


def stripe(received, weight, bias, taps, lepe_bias, per, qb, first, n_seq):
    peers = received.shape[0]
    length = peers * per
    return pl.pallas_call(
        functools.partial(stripe_kernel, first, n_seq, per, qb),
        out_shape=jax.ShapeDtypeStruct((peers, HALF, n_seq * per), BF16),
        in_specs=[VMEM] * 5,
        out_specs=VMEM,
        scratch_shapes=[
            pltpu.VMEM((n_seq, length, LANES), BF16),
            pltpu.VMEM((n_seq, length, LANES), BF16),
            pltpu.VMEM((n_seq, HEADS, 32, length), BF16),
            pltpu.VMEM((n_seq, length + 16, LANES), F32),
            pltpu.VMEM((n_seq, length, LANES), F32),
        ],
        compiler_params=pltpu.CompilerParams(vmem_limit_bytes=44 * 2**20),
        cost_estimate=pl.CostEstimate(
            flops=4 * HEADS * n_seq * length * length * 256,
            bytes_accessed=4 * 10**6,
            transcendentals=HEADS * n_seq * length * length,
        ),
        name="stripe",
    )(received, weight, bias, taps, lepe_bias)


def tail_kernel(cuts, x_ref, row_ref, *refs):
    cols = refs[: len(cuts)]
    (eye_ref, wr_ref, wc_ref, vec_ref, f1_ref, f1b_ref, f2_ref, out_ref, col_s) = refs[len(cuts) :]
    rows, chans, tile_w = x_ref.shape
    each = row_ref.shape[2] // tile_w
    peers = cols[0].shape[0]
    tile_h = rows * pl.num_programs(0)
    per = tile_w // peers

    @pl.when(pl.program_id(0) == 0)
    def _():
        for (first, count), col_ref in zip(cuts, cols):
            for p in range(peers):
                y = lax.dot_general(col_ref[p], eye_ref[...], TN, preferred_element_type=F32)
                for j in range(count):
                    dst = pl.ds(p * per + first + j, tile_h, stride=tile_w)
                    col_s[dst, :] = y[j * tile_h : (j + 1) * tile_h]

    pb, gain, bias, f2b = [columns(vec_ref[i : i + 1], tile_w) for i in range(4)]
    resids, turned = [], []
    count = rows * tile_w
    both = col_s[pl.ds(pl.multiple_of(pl.program_id(0) * count, count), count), :].astype(BF16)
    for i in range(rows):
        col = both[i * tile_w : (i + 1) * tile_w]
        row = row_ref[i // each][:, i % each * tile_w : (i % each + 1) * tile_w]
        resid = (
            x_ref[i].astype(F32)
            + jnp.dot(wr_ref[...], row, preferred_element_type=F32)
            + lax.dot_general(wc_ref[...], col, NT, preferred_element_type=F32)
            + pb
        )
        turned.append(norm_channels(resid, gain, bias).T.astype(BF16))
        resids.append(resid + f2b)
    normed = jnp.concatenate(turned, axis=0)
    hidden = jnp.dot(normed, f1_ref[...], preferred_element_type=F32) + f1b_ref[...]
    hidden = (0.5 * hidden * (1.0 + lax.erf(hidden * (0.5**0.5)))).astype(BF16)
    out = jnp.dot(hidden, f2_ref[...], preferred_element_type=F32)
    for i in range(rows):
        piece = out[i * tile_w : (i + 1) * tile_w].T
        out_ref[i] = (resids[i] + piece).astype(BF16)


def tail(tokens, row, cuts, cols, proj_w, proj_b, gain, bias, fc1_w, fc1_b, fc2_w, fc2_b):
    tile_h, chans, tile_w = tokens.shape
    each = row.shape[2] // tile_w
    rows = 16 if 16 % each == 0 else each
    ffn = fc1_w.shape[1]
    full = lambda a: pl.BlockSpec(a.shape, lambda i: (0,) * a.ndim)
    block = lambda d: pl.BlockSpec((rows, d, tile_w), lambda i: (i, 0, 0))
    proj_t = proj_w.T
    consts = [
        jnp.eye(HALF, LANES, dtype=BF16), proj_t[:, :HALF],
        jnp.pad(proj_t[:, HALF:], ((0, 0), (0, LANES - HALF))),
        jnp.stack([proj_b, gain, bias, fc2_b]), fc1_w, fc1_b[None], fc2_w,
    ]
    return pl.pallas_call(
        functools.partial(tail_kernel, cuts),
        grid=(tile_h // rows,),
        out_shape=jax.ShapeDtypeStruct(tokens.shape, BF16),
        in_specs=[block(chans), pl.BlockSpec((rows // each,) + row.shape[1:], lambda i: (i, 0, 0))]
        + [full(a) for a in cols] + [full(a) for a in consts],
        out_specs=block(chans),
        scratch_shapes=[pltpu.VMEM((tile_h * tile_w, LANES), F32)],
        compiler_params=pltpu.CompilerParams(vmem_limit_bytes=44 * 2**20),
        cost_estimate=pl.CostEstimate(
            flops=2 * tile_h * tile_w * chans * (chans + 2 * ffn),
            bytes_accessed=8 * 10**6,
            transcendentals=tile_h * tile_w * ffn,
        ),
        name="tail",
    )(tokens, row, *cols, *consts)


def shards(
    tokens, norm1_gain, norm1_bias, qkv_weight, qkv_bias, lepe_taps, lepe_bias, proj_weight,
    proj_bias, norm2_gain, norm2_bias, fc1_weight, fc1_bias, fc2_weight, fc2_bias,
):
    tokens = jnp.swapaxes(tokens, 1, 2)
    tile_h, chans, tile_w = tokens.shape
    n_rows = lax.axis_size("rows")
    n_cols = lax.axis_size("cols")

    def branch(which):
        lo = which * HALF
        lanes = lambda a: jnp.pad(a, [(0, 0)] * (a.ndim - 1) + [(0, LANES - HALF)])
        cut = lambda a: jnp.concatenate(
            [lanes(a[..., b * chans + lo : b * chans + lo + HALF]) for b in range(3)], axis=-1
        )
        return (
            cut(qkv_weight),
            cut(qkv_bias)[None],
            lanes(lepe_taps[:, lo : lo + HALF]),
            lanes(lepe_bias[lo : lo + HALF])[None],
        )

    swap = lambda a, axis: lax.all_to_all(a, axis, split_axis=0, concat_axis=0, tiled=True)
    norm1 = (tokens, norm1_gain, norm1_bias)
    turned = [pltpu.VMEM((tile_w, tile_h, 2 * LANES), F32)]
    row_in = swap(pack(pack_rows_kernel, [], "pack_rows", *norm1, n_cols), "cols")
    col_in = swap(pack(pack_cols_kernel, turned, "pack_cols", *norm1, n_rows), "rows")
    rows = stripe(row_in, *branch(0), tile_w, n_cols * tile_w // 2, 0, tile_h // n_cols)
    rows = swap(rows, "cols")
    cuts = ((0, tile_w // n_rows),)
    cols = [
        swap(stripe(col_in, *branch(1), tile_h, n_rows * tile_h, *cut), "rows") for cut in cuts
    ]
    out = tail(
        tokens, rows, cuts, cols, proj_weight, proj_bias, norm2_gain, norm2_bias,
        fc1_weight, fc1_bias, fc2_weight, fc2_bias,
    )
    return jnp.swapaxes(out, 1, 2)


def solution(mesh):
    in_specs = (P("rows", "cols", None),) + (P(),) * 14
    return jax.shard_map(
        shards, mesh=mesh, in_specs=in_specs, out_specs=P("rows", "cols", None), check_vma=False
    )
```

time: 225 us -> 193 us (0.86)
  Pallas kernels: 133 us -> 103 us
  local copies, waits for them, and re-layouts: 25.5 us -> 12 us
  waiting for transfers between devices: 27.4 us -> 39.2 us
    pallas_call x5, Pallas kernels: 133 us -> 103 us  [the longest x2 80.9 us: stripe(): pl.pallas_call(functools.partial(stripe_kernel, first, n_seq, per, qb), o...]
    all_to_all x4, waiting for transfers between devices: 27.4 us -> 39.2 us  [shards(): lax.all_to_all(a, axis, split_axis=0, concat_axis=0, tiled=True)]
    unnamed x29 -> x48, local copies, waits for them, and re-layouts: 15 us -> 9.72 us
    pallas_call x1 -> x0, local copies, waits for them, and re-layouts: 4.6 us -> none  [tail(): pl.pallas_call(tail_kernel, grid=(peers,), out_shape=jax.ShapeDtypeStruct...]
    reshape x2 -> x0, local copies, waits for them, and re-layouts: 2.82 us -> none  [the longest x1 1.41 us: pack(): gain.reshape(chans, 1)]
  transfers between devices with their start and end apart: 4 -> 4, of which waited for: 2 -> 2; matrix products, arithmetic and copies ran while one was open for 6% -> 4% of each run, Pallas kernels for 44% -> 45%
where the time goes in v1:
time: 193 us; the launch traced here: 192 us
  Pallas kernels  103 us (53%)
  waiting for transfers between devices  39.2 us (20%)
  starting transfers between devices  33.2 us (17%)
  local copies, waits for them, and re-layouts  12 us (6%)
  other arithmetic  4.25 us (2%)
    pallas_call x2, Pallas kernels, stripe(): pl.pallas_call(functools.partial(stripe_kernel, first, n_seq, per, qb), o...  80.9 us
    all_to_all x4, waiting for transfers between devices, shards(): lax.all_to_all(a, axis, split_axis=0, concat_axis=0, tiled=True)  39.2 us
    all_to_all x4, starting transfers between devices, shards(): lax.all_to_all(a, axis, split_axis=0, concat_axis=0, tiled=True)  33.2 us
    pallas_call x1, Pallas kernels, tail(): pl.pallas_call(functools.partial(tail_kernel, cuts), grid=(tile_h // rows...  13.2 us
    unnamed x48, local copies, waits for them, and re-layouts  9.72 us
    pallas_call x2, Pallas kernels, pack(): pl.pallas_call(kernel, out_shape=jax.ShapeDtypeStruct((peers, chans, rows...  9 us
  transfers between devices with their start and end apart: 4, of which 2 were waited for; matrix products, arithmetic and copies ran while one was open for 4% of the time, Pallas kernels for 45%

profile of v1, /device:TPU:8, one launch (start us, length us, event | category | flops | bytes accessed | tf_op | source)
XLA Modules:
  0.0 192.1 jit_solution(17797294572891428647)
XLA Ops:
  0.0 0.0 copy-start.3
  0.0 1.7 copy-done.3
  1.7 0.0 copy-start.7
  1.7 0.7 copy-done.7
  2.3 0.7 copy-done.9
  3.0 3.9 %pack_rows.1 = bf16[16,144,384]{2,1,0:T(8,128)(2,1)} custom-call(bf16[64,144,96]{2,1,0:T(8,128)(2,1)S(1)} %bitcast.13, f32[1,144]{1,0:T(1,128)S(1)} %bitcast.16, f32[1,144]{1,0:T(1,128)S(1)} %bitcast.18), custom_call_target="tpu_custom_call" | custom-call | flops 10000000000 | bytes 5000000 | tf_op jit(solution)/shard_map/pack_rows/pallas_call | solution.py:88
  6.9 0.0 copy-start.15
  6.9 0.0 copy-start.14
  6.9 0.0 copy-start.22
  6.9 0.0 copy-start.11
  6.9 0.0 copy-start.8
  6.9 0.0 copy-start.10
  6.9 6.0 %all-to-all-start = ((bf16[16,144,384]{2,1,0:T(8,128)(2,1)}), bf16[16,144,384]{2,1,0:T(8,128)(2,1)S(1)}, u32[]{:S(2)}, u32[]{:S(2)}) async-start(bf16[16,144,384]{2,1,0:T(8,128)(2,1)} %pack_rows.1), calls=%async_computation | async-start | bytes 3538944 | tf_op jit(solution)/shard_map/all_to_all | solution.py:313
  12.9 0.0 copy-done.15
  12.9 0.6 fusion.14
  13.5 0.0 copy-done.14
  13.5 0.0 copy-done.22
  13.5 0.0 copy-done.11
  13.6 0.6 slice_select_fusion
  14.2 0.8 fusion.12
  15.0 0.0 copy-done.8
  15.0 0.0 copy-done.10
  15.0 0.0 copy-start.4
  15.0 1.7 copy-done.4
  16.6 5.1 %pack_cols.1 = bf16[16,144,384]{2,1,0:T(8,128)(2,1)S(1)} custom-call(bf16[64,144,96]{2,1,0:T(8,128)(2,1)S(1)} %bitcast.14, f32[1,144]{1,0:T(1,128)S(1)} %bitcast.17, f32[1,144]{1,0:T(1,128)S(1)} %bitcast.19), custom_call_target="tpu_custom_call" | custom-call | flops 10000000000 | bytes 5000000 | tf_op jit(solution)/shard_map/pack_cols/pallas_call | solution.py:88
  21.8 0.0 copy-start
  21.8 1.2 copy-done
  23.0 12.6 %all-to-all-done.x_ref = bf16[16,144,384]{2,1,0:T(8,128)(2,1)S(1)} async-done(((bf16[16,144,384]{2,1,0:T(8,128)(2,1)}), bf16[16,144,384]{2,1,0:T(8,128)(2,1)S(1)}, u32[]{:S(2)}, u32[]{:S(2)}) %all-to-all-start) | async-done | bytes 1769504 | tf_op jit(solution)/shard_map/all_to_all | solution.py:313
  35.6 10.7 %all-to-all-start.2 = ((bf16[16,144,384]{2,1,0:T(8,128)(2,1)}), bf16[16,144,384]{2,1,0:T(8,128)(2,1)S(1)}, u32[]{:S(2)}, u32[]{:S(2)}) async-start(bf16[16,144,384]{2,1,0:T(8,128)(2,1)} %copy-done), calls=%async_computation.2 | async-start | bytes 3538944 | tf_op jit(solution)/shard_map/all_to_all | solution.py:313
  46.3 0.6 select_maximum_fusion
  47.0 0.7 slice.73
  47.7 0.0 copy-done.16
  47.7 0.1 slice.72
  47.8 0.8 fusion.7.w_ref
  48.6 1.5 fusion.9.w_ref
  50.1 0.7 slice_select_fusion.1.taps_ref
  50.8 45.9 %stripe.2 = bf16[16,72,384]{2,1,0:T(8,128)(2,1)S(1)} custom-call(bf16[16,144,384]{2,1,0:T(8,128)(2,1)S(1)} %all-to-all-done.x_ref, bf16[144,384]{1,0:T(8,128)(2,1)S(1)} %fusion.7.w_ref, f32[1,384]{1,0:T(1,128)S(1)} %broadcast_in_dim.25.b_ref, f32[3,128]{1,0:T(4,128)S(1)} %slice_select_fusion.1.taps_ref, f32[1,128]{1,0:T(1,128)S(1)} %get-tuple-element.17.lb_ref), custom_call_target="tpu_custom_call" | custom-call | flops 28991029248 | bytes 4000000 | tf_op jit(solution)/shard_map/stripe/pallas_call | solution.py:196
  96.7 0.0 copy-start.1
  96.7 0.9 copy-done.1
  97.6 0.0 all-to-all-done.2.x_ref
  97.6 6.6 %all-to-all-start.1 = ((bf16[16,72,384]{2,1,0:T(8,128)(2,1)}), bf16[16,72,384]{2,1,0:T(8,128)(2,1)S(1)}, u32[]{:S(2)}, u32[]{:S(2)}) async-start(bf16[16,72,384]{2,1,0:T(8,128)(2,1)} %copy-done.1), calls=%async_computation.1 | async-start | bytes 1769472 | tf_op jit(solution)/shard_map/all_to_all | solution.py:313
  104.2 0.0 copy-start.2
  104.2 0.9 copy-done.2
  105.0 35.0 %stripe.3 = bf16[16,72,384]{2,1,0:T(8,128)(2,1)} custom-call(bf16[16,144,384]{2,1,0:T(8,128)(2,1)S(1)} %all-to-all-done.2.x_ref, bf16[144,384]{1,0:T(8,128)(2,1)S(1)} %copy-done.2, f32[1,384]{1,0:T(1,128)S(1)} %broadcast_in_dim.27.b_ref, f32[3,128]{1,0:T(4,128)S(1)} %pad.68.taps_ref, f32[1,128]{1,0:T(1,128)S(1)} %pad_bitcast_fusion.lb_ref), custom_call_target="tpu_custom_call" | custom-call | flops 19327352832 | bytes 4000000 | tf_op jit(solution)/shard_map/stripe/pallas_call | solution.py:196
  140.1 0.0 copy-start.19
  140.1 0.0 copy-start.20
  140.1 0.0 copy-start.21
  140.1 0.0 copy-start.6
  140.1 0.0 all-to-all-done.1.row_ref
  140.1 9.9 %all-to-all-start.3 = ((bf16[16,72,384]{2,1,0:T(8,128)(2,1)}), bf16[16,72,384]{2,1,0:T(8,128)(2,1)S(1)}, u32[]{:S(2)}, u32[]{:S(2)}) async-start(bf16[16,72,384]{2,1,0:T(8,128)(2,1)} %stripe.3), calls=%async_computation.3 | async-start | bytes 1769472 | tf_op jit(solution)/shard_map/all_to_all | solution.py:313
  150.1 0.0 copy-done.13
  150.1 0.1 copy.16
  150.2 0.0 copy-done.17
  150.2 0.0 copy-done.12
  150.2 0.2 copy.17.refs_7_
  150.4 0.1 fusion.13
  150.5 0.0 copy-done.18
  150.5 0.0 copy-done.19
  150.5 0.0 copy-done.20
  150.5 0.0 copy-done.21
  150.6 26.7 %all-to-all-done.3.refs_0_ = bf16[16,72,384]{2,1,0:T(8,128)(2,1)S(1)} async-done(((bf16[16,72,384]{2,1,0:T(8,128)(2,1)}), bf16[16,72,384]{2,1,0:T(8,128)(2,1)S(1)}, u32[]{:S(2)}, u32[]{:S(2)}) %all-to-all-start.3) | async-done | bytes 884768 | tf_op jit(solution)/shard_map/all_to_all | solution.py:313
  177.2 0.0 copy-done.6
  177.2 1.7 copy-done.5
  178.9 13.2 %tail.1 = bf16[64,144,96]{2,1,0:T(8,128)(2,1)} custom-call(bf16[64,144,96]{2,1,0:T(8,128)(2,1)S(1)} %bitcast.15, bf16[16,72,384]{2,1,0:T(8,128)(2,1)S(1)} %all-to-all-done.1.row_ref, bf16[16,72,384]{2,1,0:T(8,128)(2,1)S(1)} %all-to-all-done.3.refs_0_, bf16[72,128]{1,0:T(8,128)(2,1)S(1)} %fusion.10.refs_1_, bf16[144,72]{1,0:T(8,128)(2,1)S(1)} %get-tuple-element.11.refs_2_, ...), custom_call_target="tpu_custom_call" | custom-call | flops 2293235712 | bytes 8000000 | tf_op jit(solution)/shard_map/tail/pallas_call | solution.py:273
  (17 shorter events, 0.1 us)
Async XLA Ops:
  0.0 1.7 copy-start.3
  1.7 0.7 copy-start.7
  2.3 0.7 copy-start.9
  6.9 6.0 %copy-start.15 = (f32[432]{0:T(512)S(1)}, f32[432]{0:T(512)}, u32[]{:S(2)}) copy-start(f32[432]{0:T(512)} %param.19) | copy-start | bytes 5188
  6.9 6.6 %copy-start.14 = (pred[128]{0:T(512)(128)(4,1)S(1)}, pred[128]{0:T(512)(128)(4,1)}, u32[]{:S(2)}) copy-start(pred[128]{0:T(512)(128)(4,1)} %constant.7.clone.1) | copy-start | bytes 388
  6.9 6.6 %copy-start.22 = (f32[144]{0:T(256)S(1)}, f32[144]{0:T(256)}, u32[]{:S(2)}) copy-start(f32[144]{0:T(256)} %param.21) | copy-start | bytes 1732
  6.9 6.7 %copy-start.11 = (bf16[144,432]{1,0:T(8,128)(2,1)S(1)}, bf16[144,432]{1,0:T(8,128)(2,1)}, u32[]{:S(2)}) copy-start(bf16[144,432]{1,0:T(8,128)(2,1)} %param.18) | copy-start | bytes 373252
  6.9 8.1 %copy-start.8 = (f32[144]{0:T(256)S(1)}, f32[144]{0:T(256)}, u32[]{:S(2)}) copy-start(f32[144]{0:T(256)} %param.16) | copy-start | bytes 1732
  6.9 8.1 %copy-start.10 = (f32[144]{0:T(256)S(1)}, f32[144]{0:T(256)}, u32[]{:S(2)}) copy-start(f32[144]{0:T(256)} %param.17) | copy-start | bytes 1732
  6.9 28.7 %all-to-all-start = ((bf16[16,144,384]{2,1,0:T(8,128)(2,1)}), bf16[16,144,384]{2,1,0:T(8,128)(2,1)S(1)}, u32[]{:S(2)}, u32[]{:S(2)}) async-start(bf16[16,144,384]{2,1,0:T(8,128)(2,1)} %pack_rows.1), calls=%async_computation | async-start | bytes 3538944 | tf_op jit(solution)/shard_map/all_to_all | solution.py:313
  15.0 1.7 copy-start.4
  21.8 1.2 copy-start
  23.0 24.7 %copy-start.16 = (f32[3,144]{1,0:T(4,128)S(1)}, f32[3,144]{1,0:T(4,128)}, u32[]{:S(2)}) copy-start(f32[3,144]{1,0:T(4,128)} %param.20) | copy-start | bytes 5188
  35.6 62.0 %all-to-all-start.2 = ((bf16[16,144,384]{2,1,0:T(8,128)(2,1)}), bf16[16,144,384]{2,1,0:T(8,128)(2,1)S(1)}, u32[]{:S(2)}, u32[]{:S(2)}) async-start(bf16[16,144,384]{2,1,0:T(8,128)(2,1)} %copy-done), calls=%async_computation.2 | async-start | bytes 3538944 | tf_op jit(solution)/shard_map/all_to_all | solution.py:313
  96.7 0.9 copy-start.1
  97.6 42.5 %all-to-all-start.1 = ((bf16[16,72,384]{2,1,0:T(8,128)(2,1)}), bf16[16,72,384]{2,1,0:T(8,128)(2,1)S(1)}, u32[]{:S(2)}, u32[]{:S(2)}) async-start(bf16[16,72,384]{2,1,0:T(8,128)(2,1)} %copy-done.1), calls=%async_computation.1 | async-start | bytes 1769472 | tf_op jit(solution)/shard_map/all_to_all | solution.py:313
  104.2 0.9 copy-start.2
  140.1 10.0 %copy-start.13 = (bf16[144,144]{1,0:T(8,128)(2,1)S(1)}, bf16[144,144]{1,0:T(8,128)(2,1)}, u32[]{:S(2)}) copy-start(bf16[144,144]{1,0:T(8,128)(2,1)} %param.22) | copy-start | bytes 124420
  140.1 10.1 %copy-start.17 = (f32[576]{0:T(1024)S(1)}, f32[576]{0:T(1024)}, u32[]{:S(2)}) copy-start(f32[576]{0:T(1024)} %param.27) | copy-start | bytes 6916
  140.1 10.1 %copy-start.12 = (bf16[576,144]{0,1:T(8,128)(2,1)S(1)}, bf16[576,144]{0,1:T(8,128)(2,1)}, u32[]{:S(2)}) copy-start(bf16[576,144]{0,1:T(8,128)(2,1)} %param.28) | copy-start | bytes 497668
  140.1 10.4 %copy-start.18 = (f32[144]{0:T(256)S(1)}, f32[144]{0:T(256)}, u32[]{:S(2)}) copy-start(f32[144]{0:T(256)} %param.29) | copy-start | bytes 1732
  140.1 10.4 %copy-start.19 = (f32[144]{0:T(256)S(1)}, f32[144]{0:T(256)}, u32[]{:S(2)}) copy-start(f32[144]{0:T(256)} %param.25) | copy-start | bytes 1732
  140.1 10.4 %copy-start.20 = (f32[144]{0:T(256)S(1)}, f32[144]{0:T(256)}, u32[]{:S(2)}) copy-start(f32[144]{0:T(256)} %param.24) | copy-start | bytes 1732
  140.1 10.4 %copy-start.21 = (f32[144]{0:T(256)S(1)}, f32[144]{0:T(256)}, u32[]{:S(2)}) copy-start(f32[144]{0:T(256)} %param.23) | copy-start | bytes 1732
  140.1 37.1 %copy-start.6 = (bf16[144,576]{1,0:T(8,128)(2,1)S(1)}, bf16[144,576]{1,0:T(8,128)(2,1)}, u32[]{:S(2)}) copy-start(bf16[144,576]{1,0:T(8,128)(2,1)} %refs_5_.1) | copy-start | bytes 497668
  140.1 37.1 %all-to-all-start.3 = ((bf16[16,72,384]{2,1,0:T(8,128)(2,1)}), bf16[16,72,384]{2,1,0:T(8,128)(2,1)S(1)}, u32[]{:S(2)}, u32[]{:S(2)}) async-start(bf16[16,72,384]{2,1,0:T(8,128)(2,1)} %stripe.3), calls=%async_computation.3 | async-start | bytes 1769472 | tf_op jit(solution)/shard_map/all_to_all | solution.py:313
  177.2 1.7 copy-start.5

commit v2 on v1

--- a/solution.py
+++ b/solution.py
@@ -20,6 +20,7 @@
 NT = (((1,), (1,)), ((), ()))
 TN = (((0,), (0,)), ((), ()))
 VMEM = pl.BlockSpec(memory_space=pltpu.VMEM)
+MESH = pl.DeviceIdType.MESH
 
 
 def columns(row, lanes):
@@ -97,6 +98,75 @@
         ),
         name=name,
     )(tokens, gain[None], bias[None])
+
+
+def swap_kernel(axis, x_ref, out_ref, send_sem, recv_sem, own_sem):
+    peers = lax.axis_size(axis)
+    me = lax.axis_index(axis)
+    barrier = pltpu.get_barrier_semaphore()
+
+    def greet(k, _):
+        peer = lax.rem(me + k, peers)
+        pl.semaphore_signal(barrier, inc=1, device_id={axis: peer}, device_id_type=MESH)
+        return 0
+
+    lax.fori_loop(1, peers, greet, 0)
+    pl.semaphore_wait(barrier, peers - 1)
+
+    def copy(k):
+        peer = lax.rem(me + k, peers)
+        return pltpu.make_async_remote_copy(
+            src_ref=x_ref.at[peer],
+            dst_ref=out_ref.at[me],
+            send_sem=send_sem.at[k],
+            recv_sem=recv_sem.at[k],
+            device_id={axis: peer},
+            device_id_type=MESH,
+        )
+
+    def arrival(k):
+        peer = lax.rem(me + peers - k, peers)
+        return pltpu.make_async_remote_copy(
+            src_ref=x_ref.at[peer],
+            dst_ref=out_ref.at[peer],
+            send_sem=send_sem.at[k],
+            recv_sem=recv_sem.at[k],
+            device_id={axis: peer},
+            device_id_type=MESH,
+        )
+
+    def start(k, _):
+        copy(k).start()
+        return 0
+
+    def finish(k, _):
+        copy(k).wait_send()
+        arrival(k).wait_recv()
+        return 0
+
+    lax.fori_loop(1, peers, start, 0)
+    own = pltpu.make_async_copy(x_ref.at[me], out_ref.at[me], own_sem)
+    own.start()
+    own.wait()
+    lax.fori_loop(1, peers, finish, 0)
+
+
+def swap_blocks(x, axis, collective_id):
+    peers = x.shape[0]
+    return pl.pallas_call(
+        functools.partial(swap_kernel, axis),
+        out_shape=jax.ShapeDtypeStruct(x.shape, x.dtype),
+        in_specs=[pl.BlockSpec(memory_space=pl.ANY)],
+        out_specs=pl.BlockSpec(memory_space=pl.ANY),
+        scratch_shapes=[
+            pltpu.SemaphoreType.DMA((peers,)),
+            pltpu.SemaphoreType.DMA((peers,)),
+            pltpu.SemaphoreType.DMA,
+        ],
+        compiler_params=pltpu.CompilerParams(collective_id=collective_id, has_side_effects=True),
+        cost_estimate=pl.CostEstimate(flops=2 * 10**10, bytes_accessed=4 * 10**6, transcendentals=0),
+        name="swap_blocks",
+    )(x)
 
 
 def stripe_kernel(
@@ -184,18 +254,19 @@
 
     def send(d, _):
         at = pl.ds(pl.multiple_of(d * per, 16), per)
-        out_ref[d] = m_s[:, at, :].reshape(n_seq * per, LANES).T[:HALF].astype(BF16)
+        x = m_s[:, at, :].reshape(n_seq * per, LANES)
+        out_ref[d] = x.T[: out_ref.shape[1]].astype(BF16)
         return 0
 
     lax.fori_loop(0, peers, send, 0, unroll=UNROLL)
 
 
-def stripe(received, weight, bias, taps, lepe_bias, per, qb, first, n_seq):
+def stripe(received, weight, bias, taps, lepe_bias, per, qb, first, n_seq, keep=HALF):
     peers = received.shape[0]
     length = peers * per
     return pl.pallas_call(
         functools.partial(stripe_kernel, first, n_seq, per, qb),
-        out_shape=jax.ShapeDtypeStruct((peers, HALF, n_seq * per), BF16),
+        out_shape=jax.ShapeDtypeStruct((peers, keep, n_seq * per), BF16),
         in_specs=[VMEM] * 5,
         out_specs=VMEM,
         scratch_shapes=[
@@ -239,7 +310,7 @@
     both = col_s[pl.ds(pl.multiple_of(pl.program_id(0) * count, count), count), :].astype(BF16)
     for i in range(rows):
         col = both[i * tile_w : (i + 1) * tile_w]
-        row = row_ref[i // each][:, i % each * tile_w : (i % each + 1) * tile_w]
+        row = row_ref[i // each][:HALF, i % each * tile_w : (i % each + 1) * tile_w]
         resid = (
             x_ref[i].astype(F32)
             + jnp.dot(wr_ref[...], row, preferred_element_type=F32)
@@ -313,14 +384,17 @@
     swap = lambda a, axis: lax.all_to_all(a, axis, split_axis=0, concat_axis=0, tiled=True)
     norm1 = (tokens, norm1_gain, norm1_bias)
     turned = [pltpu.VMEM((tile_w, tile_h, 2 * LANES), F32)]
-    row_in = swap(pack(pack_rows_kernel, [], "pack_rows", *norm1, n_cols), "cols")
     col_in = swap(pack(pack_cols_kernel, turned, "pack_cols", *norm1, n_rows), "rows")
-    rows = stripe(row_in, *branch(0), tile_w, n_cols * tile_w // 2, 0, tile_h // n_cols)
-    rows = swap(rows, "cols")
+    row_out = pack(pack_rows_kernel, [], "pack_rows", *norm1, n_cols)
+    row_out, col_in = lax.optimization_barrier((row_out, col_in))
+    row_in = swap(row_out, "cols")
     cuts = ((0, tile_w // n_rows),)
-    cols = [
-        swap(stripe(col_in, *branch(1), tile_h, n_rows * tile_h, *cut), "rows") for cut in cuts
-    ]
+    cols = [stripe(col_in, *branch(1), tile_h, n_rows * tile_h, *cut) for cut in cuts]
+    cols, row_in = lax.optimization_barrier((cols, row_in))
+    cols = [swap(part, "rows") for part in cols]
+    rows = stripe(row_in, *branch(0), tile_w, n_cols * tile_w // 2, 0, tile_h // n_cols, 80)
+    rows, cols = lax.optimization_barrier((rows, cols))
+    rows = swap_blocks(rows, "cols", 1)
     out = tail(
         tokens, rows, cuts, cols, proj_weight, proj_bias, norm2_gain, norm2_bias,
         fc1_weight, fc1_bias, fc2_weight, fc2_bias,

time: 193 us -> 198 us (1.026)
  the two profiles are of different devices: /device:TPU:8 before, /device:TPU:31 now
where the time goes in v2:
time: 198 us; the launch traced here: 197 us
  Pallas kernels  123 us (62%)
  starting transfers between devices  27.2 us (14%)
  waiting for transfers between devices  27 us (14%)
  local copies, waits for them, and re-layouts  17.1 us (9%)
  other arithmetic  2.59 us (1%)
    pallas_call x2, Pallas kernels, stripe(): pl.pallas_call(functools.partial(stripe_kernel, first, n_seq, per, qb), o...  80.2 us
    all_to_all x3, starting transfers between devices, shards(): lax.all_to_all(a, axis, split_axis=0, concat_axis=0, tiled=True)  27.2 us
    all_to_all x3, waiting for transfers between devices, shards(): lax.all_to_all(a, axis, split_axis=0, concat_axis=0, tiled=True)  27 us
    pallas_call x1, Pallas kernels, swap_blocks(): pl.pallas_call(functools.partial(swap_kernel, axis), out_shape=jax.ShapeD...  19.2 us
    pallas_call x1, Pallas kernels, tail(): pl.pallas_call(functools.partial(tail_kernel, cuts), grid=(tile_h // rows...  14.3 us
    unnamed x70, local copies, waits for them, and re-layouts  13.9 us
    pallas_call x2, Pallas kernels, pack(): pl.pallas_call(kernel, out_shape=jax.ShapeDtypeStruct((peers, chans, rows...  9.03 us
  transfers between devices with their start and end apart: 3, of which 1 were waited for; matrix products, arithmetic and copies ran while one was open for 3% of the time, Pallas kernels for 42%

profile of v2, /device:TPU:31, one launch (start us, length us, event | category | flops | bytes accessed | tf_op | source)
XLA Modules:
  0.0 197.0 jit_solution(16250294217115971960)
XLA Ops:
  0.0 1.7 copy-done.11
  1.7 0.7 copy-done.15
  2.3 0.7 copy-done.17
  3.0 6.4 %pack_cols.1 = bf16[16,144,384]{2,1,0:T(8,128)(2,1)} custom-call(bf16[64,144,96]{2,1,0:T(8,128)(2,1)S(1)} %bitcast.13, f32[1,144]{1,0:T(1,128)S(1)} %bitcast.16, f32[1,144]{1,0:T(1,128)S(1)} %bitcast.18), custom_call_target="tpu_custom_call" | custom-call | flops 10000000000 | bytes 5000000 | tf_op jit(solution)/shard_map/pack_cols/pallas_call | solution.py:89
  9.4 0.0 copy-start.24
  9.4 0.0 copy-start.23
  9.4 0.0 copy-start.28
  9.4 0.0 copy-start.29
  9.5 0.0 copy-start.30
  9.5 0.0 copy-start.31
  9.5 0.0 copy-start.32
  9.5 0.0 copy-start.22
  9.5 11.0 %all-to-all-start = ((bf16[16,144,384]{2,1,0:T(8,128)(2,1)}), bf16[16,144,384]{2,1,0:T(8,128)(2,1)S(1)}, u32[]{:S(2)}, u32[]{:S(2)}) async-start(bf16[16,144,384]{2,1,0:T(8,128)(2,1)} %pack_cols.1), calls=%async_computation | async-start | bytes 3538944 | tf_op jit(solution)/shard_map/all_to_all | solution.py:384
  20.5 0.0 copy-done.26
  20.5 0.0 copy-start.16
  20.6 0.0 copy-start.18
  20.6 0.1 fusion.14
  20.7 0.6 broadcast_in_dim.25.b_ref
  21.2 0.0 copy-done.27
  21.2 0.1 slice.64
  21.3 0.0 copy-done.33
  21.3 0.1 slice.65
  21.4 0.6 select_bitcast_fusion
  22.0 0.6 broadcast_in_dim.27.b_ref
  22.6 0.1 copy.16
  22.7 0.0 copy-done.23
  22.7 0.9 copy.17.refs_7_
  23.6 0.6 fusion.13
  24.2 0.6 pad.70.refs_3_
  24.8 0.5 pad_bitcast_fusion.lb_ref
  25.4 0.6 fusion.10.refs_1_
  26.0 0.1 fusion.12
  26.1 0.7 fusion.7.w_ref
  26.8 0.7 fusion.9.w_ref
  27.5 0.0 copy-done.16
  27.5 0.0 copy-start.12
  27.5 1.7 copy-done.12
  29.1 2.7 %pack_rows.1 = bf16[16,144,384]{2,1,0:T(8,128)(2,1)S(1)} custom-call(bf16[64,144,96]{2,1,0:T(8,128)(2,1)S(1)} %bitcast.14, f32[1,144]{1,0:T(1,128)S(1)} %bitcast.17, f32[1,144]{1,0:T(1,128)S(1)} %bitcast.19), custom_call_target="tpu_custom_call" | custom-call | flops 10000000000 | bytes 5000000 | tf_op jit(solution)/shard_map/pack_rows/pallas_call | solution.py:89
  31.8 0.0 copy-start
  31.8 1.2 copy-done
  33.0 27.0 %all-to-all-done.x_ref = bf16[16,144,384]{2,1,0:T(8,128)(2,1)S(1)} async-done(((bf16[16,144,384]{2,1,0:T(8,128)(2,1)}), bf16[16,144,384]{2,1,0:T(8,128)(2,1)S(1)}, u32[]{:S(2)}, u32[]{:S(2)}) %all-to-all-start) | async-done | bytes 1769504 | tf_op jit(solution)/shard_map/all_to_all | solution.py:384
  60.0 9.5 %all-to-all-start.1 = ((bf16[16,144,384]{2,1,0:T(8,128)(2,1)}), bf16[16,144,384]{2,1,0:T(8,128)(2,1)S(1)}, u32[]{:S(2)}, u32[]{:S(2)}) async-start(bf16[16,144,384]{2,1,0:T(8,128)(2,1)} %copy-done), calls=%async_computation.1 | async-start | bytes 3538944 | tf_op jit(solution)/shard_map/all_to_all | solution.py:384
  69.5 0.9 copy-done.4
  70.3 0.7 copy-done.9
  71.0 0.6 copy-done.19
  71.6 34.1 %stripe.2 = bf16[16,72,384]{2,1,0:T(8,128)(2,1)S(1)} custom-call(bf16[16,144,384]{2,1,0:T(8,128)(2,1)S(1)} %all-to-all-done.x_ref, bf16[144,384]{1,0:T(8,128)(2,1)S(1)} %copy-done.4, f32[1,384]{1,0:T(1,128)S(1)} %copy-done.9, f32[3,128]{1,0:T(4,128)S(1)} %pad.60.taps_ref, f32[1,128]{1,0:T(1,128)S(1)} %copy-done.19), custom_call_target="tpu_custom_call" | custom-call | flops 19327352832 | bytes 4000000 | tf_op jit(solution)/shard_map/stripe/pallas_call | solution.py:267
  105.7 0.9 copy-done.1
  106.6 0.0 all-to-all-done.1.x_ref
  106.6 6.8 %all-to-all-start.2 = ((bf16[16,72,384]{2,1,0:T(8,128)(2,1)}), bf16[16,72,384]{2,1,0:T(8,128)(2,1)}, u32[]{:S(2)}, u32[]{:S(2)}) async-start(bf16[16,72,384]{2,1,0:T(8,128)(2,1)} %copy-done.1), calls=%async_computation.2 | async-start | bytes 1769472 | tf_op jit(solution)/shard_map/all_to_all | solution.py:384
  113.4 46.1 %stripe.3.x_ref = bf16[16,80,384]{2,1,0:T(8,128)(2,1)S(1)} custom-call(bf16[16,144,384]{2,1,0:T(8,128)(2,1)S(1)} %all-to-all-done.1.x_ref, bf16[144,384]{1,0:T(8,128)(2,1)S(1)} %copy-done.3, f32[1,384]{1,0:T(1,128)S(1)} %copy-done.8, f32[3,128]{1,0:T(4,128)S(1)} %slice_select_fusion.1.taps_ref, f32[1,128]{1,0:T(1,128)S(1)} %copy-done.10), custom_call_target="tpu_custom_call" | custom-call | flops 28991029248 | bytes 4000000 | tf_op jit(solution)/shard_map/stripe/pallas_call | solution.py:267
  159.5 0.0 copy-start.21
  159.6 0.9 copy-done.21
  160.5 0.0 copy-start.14
  160.5 0.0 all-to-all-done.2.refs_0_
  160.5 19.2 %swap_blocks.1.row_ref = bf16[16,80,384]{2,1,0:T(8,128)(2,1)} custom-call(bf16[16,80,384]{2,1,0:T(8,128)(2,1)} %copy-done.21), custom_call_target="tpu_custom_call" | custom-call | flops 20000000000 | bytes 4000000 | tf_op jit(solution)/shard_map/swap_blocks/pallas_call | solution.py:156
  179.7 0.0 copy-done.2
  179.7 0.0 copy-done.5
  179.7 0.0 copy-done.6
  179.7 0.0 copy-done.7
  179.7 0.0 copy-done.14
  179.8 0.0 copy-start.13
  179.8 1.7 copy-done.13
  181.4 1.2 copy-done.20
  182.6 14.3 %tail.1 = bf16[64,144,96]{2,1,0:T(8,128)(2,1)} custom-call(bf16[64,144,96]{2,1,0:T(8,128)(2,1)S(1)} %bitcast.15, bf16[16,80,384]{2,1,0:T(8,128)(2,1)S(1)} %copy-done.20, bf16[16,72,384]{2,1,0:T(8,128)(2,1)} %all-to-all-done.2.refs_0_, bf16[72,128]{1,0:T(8,128)(2,1)S(1)} %copy-done.7, bf16[144,72]{1,0:T(8,128)(2,1)S(1)} %copy-done.6, ...), custom_call_target="tpu_custom_call" | custom-call | flops 2293235712 | bytes 8000000 | tf_op jit(solution)/shard_map/tail/pallas_call | solution.py:344
  (38 shorter events, 0.1 us)
Async XLA Ops:
  0.0 1.7 copy-start.11
  1.7 0.7 copy-start.15
  2.3 0.7 copy-start.17
  9.4 11.1 %copy-start.26 = (f32[432]{0:T(512)S(1)}, f32[432]{0:T(512)}, u32[]{:S(2)}) copy-start(f32[432]{0:T(512)} %param.19) | copy-start | bytes 5188
  9.4 11.8 %copy-start.27 = (f32[3,144]{1,0:T(4,128)S(1)}, f32[3,144]{1,0:T(4,128)}, u32[]{:S(2)}) copy-start(f32[3,144]{1,0:T(4,128)} %param.20) | copy-start | bytes 5188
  9.4 11.9 %copy-start.33 = (f32[144]{0:T(256)S(1)}, f32[144]{0:T(256)}, u32[]{:S(2)}) copy-start(f32[144]{0:T(256)} %param.21) | copy-start | bytes 1732
  9.4 12.0 %copy-start.25 = (pred[128]{0:T(512)(128)(4,1)S(1)}, pred[128]{0:T(512)(128)(4,1)}, u32[]{:S(2)}) copy-start(pred[128]{0:T(512)(128)(4,1)} %constant.9.clone.1) | copy-start | bytes 388
  9.4 13.1 %copy-start.24 = (bf16[144,144]{1,0:T(8,128)(2,1)S(1)}, bf16[144,144]{1,0:T(8,128)(2,1)}, u32[]{:S(2)}) copy-start(bf16[144,144]{1,0:T(8,128)(2,1)} %param.22) | copy-start | bytes 124420
  9.4 13.2 %copy-start.23 = (bf16[576,144]{0,1:T(8,128)(2,1)S(1)}, bf16[576,144]{0,1:T(8,128)(2,1)}, u32[]{:S(2)}) copy-start(bf16[576,144]{0,1:T(8,128)(2,1)} %param.28) | copy-start | bytes 497668
  9.4 14.1 %copy-start.28 = (f32[576]{0:T(1024)S(1)}, f32[576]{0:T(1024)}, u32[]{:S(2)}) copy-start(f32[576]{0:T(1024)} %param.27) | copy-start | bytes 6916
  9.4 15.9 %copy-start.29 = (f32[144]{0:T(256)S(1)}, f32[144]{0:T(256)}, u32[]{:S(2)}) copy-start(f32[144]{0:T(256)} %param.29) | copy-start | bytes 1732
  9.5 15.9 %copy-start.30 = (f32[144]{0:T(256)S(1)}, f32[144]{0:T(256)}, u32[]{:S(2)}) copy-start(f32[144]{0:T(256)} %param.25) | copy-start | bytes 1732
  9.5 15.9 %copy-start.31 = (f32[144]{0:T(256)S(1)}, f32[144]{0:T(256)}, u32[]{:S(2)}) copy-start(f32[144]{0:T(256)} %param.24) | copy-start | bytes 1732
  9.5 15.8 %copy-start.32 = (f32[144]{0:T(256)S(1)}, f32[144]{0:T(256)}, u32[]{:S(2)}) copy-start(f32[144]{0:T(256)} %param.23) | copy-start | bytes 1732
  9.5 16.5 %copy-start.22 = (bf16[144,432]{1,0:T(8,128)(2,1)S(1)}, bf16[144,432]{1,0:T(8,128)(2,1)}, u32[]{:S(2)}) copy-start(bf16[144,432]{1,0:T(8,128)(2,1)} %param.18) | copy-start | bytes 373252
  9.5 50.5 %all-to-all-start = ((bf16[16,144,384]{2,1,0:T(8,128)(2,1)}), bf16[16,144,384]{2,1,0:T(8,128)(2,1)S(1)}, u32[]{:S(2)}, u32[]{:S(2)}) async-start(bf16[16,144,384]{2,1,0:T(8,128)(2,1)} %pack_cols.1), calls=%async_computation | async-start | bytes 3538944 | tf_op jit(solution)/shard_map/all_to_all | solution.py:384
  20.5 6.9 %copy-start.16 = (f32[144]{0:T(256)S(1)}, f32[144]{0:T(256)}, u32[]{:S(2)}) copy-start(f32[144]{0:T(256)} %param.16) | copy-start | bytes 1732
  20.6 6.9 %copy-start.18 = (f32[144]{0:T(256)S(1)}, f32[144]{0:T(256)}, u32[]{:S(2)}) copy-start(f32[144]{0:T(256)} %param.17) | copy-start | bytes 1732
  27.5 1.7 copy-start.12
  31.8 1.2 copy-start
  60.0 46.6 %all-to-all-start.1 = ((bf16[16,144,384]{2,1,0:T(8,128)(2,1)}), bf16[16,144,384]{2,1,0:T(8,128)(2,1)S(1)}, u32[]{:S(2)}, u32[]{:S(2)}) async-start(bf16[16,144,384]{2,1,0:T(8,128)(2,1)} %copy-done), calls=%async_computation.1 | async-start | bytes 3538944 | tf_op jit(solution)/shard_map/all_to_all | solution.py:384
  69.4 0.9 copy-start.4
  70.3 0.7 copy-start.9
  71.0 0.6 copy-start.19
  105.7 0.9 copy-start.1
  106.6 6.8 %copy-start.3 = (bf16[144,384]{1,0:T(8,128)(2,1)S(1)}, bf16[144,384]{1,0:T(8,128)(2,1)}, u32[]{:S(2)}) copy-start(bf16[144,384]{1,0:T(8,128)(2,1)} %fusion.9.w_ref) | copy-start | bytes 331780
  106.6 6.8 %copy-start.8 = (f32[1,384]{1,0:T(1,128)S(1)}, f32[1,384]{1,0:T(1,128)}, u32[]{:S(2)}) copy-start(f32[1,384]{1,0:T(1,128)} %broadcast_in_dim.27.b_ref) | copy-start | bytes 4612
  106.6 6.8 %copy-start.10 = (f32[1,128]{1,0:T(1,128)S(1)}, f32[1,128]{1,0:T(1,128)}, u32[]{:S(2)}) copy-start(f32[1,128]{1,0:T(1,128)} %get-tuple-element.29.lb_ref) | copy-start | bytes 1540
  106.6 53.9 %all-to-all-start.2 = ((bf16[16,72,384]{2,1,0:T(8,128)(2,1)}), bf16[16,72,384]{2,1,0:T(8,128)(2,1)}, u32[]{:S(2)}, u32[]{:S(2)}) async-start(bf16[16,72,384]{2,1,0:T(8,128)(2,1)} %copy-done.1), calls=%async_computation.2 | async-start | bytes 1769472 | tf_op jit(solution)/shard_map/all_to_all | solution.py:384
  159.5 0.9 copy-start.21
  160.5 19.2 %copy-start.2 = (bf16[576,144]{1,0:T(8,128)(2,1)S(1)}, bf16[576,144]{1,0:T(8,128)(2,1)}, u32[]{:S(2)}) copy-start(bf16[576,144]{1,0:T(8,128)(2,1)} %copy.17.refs_7_) | copy-start | bytes 497668
  160.5 19.2 %copy-start.5 = (bf16[144,128]{1,0:T(8,128)(2,1)S(1)}, bf16[144,128]{1,0:T(8,128)(2,1)}, u32[]{:S(2)}) copy-start(bf16[144,128]{1,0:T(8,128)(2,1)} %pad.70.refs_3_) | copy-start | bytes 110596
  160.5 19.2 %copy-start.6 = (bf16[144,72]{1,0:T(8,128)(2,1)S(1)}, bf16[144,72]{1,0:T(8,128)(2,1)}, u32[]{:S(2)}) copy-start(bf16[144,72]{1,0:T(8,128)(2,1)} %get-tuple-element.23.refs_2_) | copy-start | bytes 62212
  160.5 19.2 %copy-start.7 = (bf16[72,128]{1,0:T(8,128)(2,1)S(1)}, bf16[72,128]{1,0:T(8,128)(2,1)}, u32[]{:S(2)}) copy-start(bf16[72,128]{1,0:T(8,128)(2,1)} %fusion.10.refs_1_) | copy-start | bytes 55300
  160.5 19.2 %copy-start.14 = (bf16[144,576]{1,0:T(8,128)(2,1)S(1)}, bf16[144,576]{1,0:T(8,128)(2,1)}, u32[]{:S(2)}) copy-start(bf16[144,576]{1,0:T(8,128)(2,1)} %refs_5_.1) | copy-start | bytes 497668
  179.8 1.7 copy-start.13
  181.4 1.2 copy-start.20
